TPU v7x, 32 devices: a whole 2x2x4 slice. The times are simulated.
32 devices in a mesh: row: 2 (over y), col: 16 (over z, x, core).
Axes of the slice: x: 2, y: 2, z: 4, core: 2. Of those that a mesh axis runs over, the one named last changes fastest.
Arguments:
- tokens: bfloat16 [32, 1024, 1152], P(('row', 'col')), may hold values from -6 to 6
- lengths: int32 [32, 3], P(('row', 'col')), may hold values from 128 to 512, as said below
- condition: bfloat16 [32, 3, 1152], P(('row', 'col')), may hold values from -6 to 6
- keep_mask: int32 [32, 1024], P(('row', 'col')), may hold values 0 or 1
- group_mask: int32 [32, 3, 16], P(('row', 'col')), may hold values 0 or 1
- qkv_weight: bfloat16 [1152, 3456], P(('row', 'col')), may hold values from -0.1875 to 0.1875
- out_weight: bfloat16 [1152, 1152], P(('row', 'col')), may hold values from -1 to 1
- mod_weight: bfloat16 [1152, 6912], P(('row', 'col')), may hold values from -0.1875 to 0.1875
- out_bias: bfloat16 [1152], P(('row', 'col')), may hold values from -3 to 3
- mod_bias: bfloat16 [6912], P(('row', 'col')), may hold values from -2 to 2
- up_weight: bfloat16 [1152, 4608], P('row', 'col'), may hold values from -0.1875 to 0.1875
- up_bias: bfloat16 [4608], P(('row', 'col')), may hold values from -3 to 3
- down_weight: bfloat16 [4608, 1152], P('col', 'row'), may hold values from -0.1875 to 0.1875
- down_bias: bfloat16 [1152], P(('row', 'col')), may hold values from -3 to 3
- cotangent: bfloat16 [32, 1024, 1152], P(('row', 'col')), may hold values from -6 to 6
Outputs:
- block_out: bfloat16 [32, 1024, 1152], P(('row', 'col'))
- grad_tokens: float32 [32, 1024, 1152], P(('row', 'col'))
- grad_qkv: float32 [1152, 3456], P(('row', 'col'))
- grad_out: float32 [1152, 1152], P(('row', 'col'))
- grad_mod: float32 [1152, 6912], P(('row', 'col'))
- grad_outbias: float32 [1152], P(('row', 'col'))
- grad_modbias: float32 [6912], P(('row', 'col'))
- grad_up: float32 [1152, 4608], P('row', 'col')
- grad_upbias: float32 [4608], P(('row', 'col'))
- grad_down: float32 [4608, 1152], P('col', 'row')
- grad_downbias: float32 [1152], P(('row', 'col'))
Inputs may be any that keep to these rules, and one draw needn't show every extreme that they name: The 3 crop lengths of a packed row sum to at most 1024; the rest of the row is padding. Some row has a crop of exactly 512 tokens and some row a crop of exactly 128.
All inputs are finite; a program needn't handle non-finite values. No bound on the sum of `keep_mask` or of `group_mask` on one device may be relied on, other than what follows from the above.
Results may differ from a plain program's by a relative error of at most 0.015.
The roundings to bfloat16 on the way count: a program that leaves them out, or rounds other values in their place, can miss the bound.
Values may be sent and summed in bfloat16 or wider, within the bound.
A program may use at most 512 MiB of HBM per device.

v0:
```python
import jax
import jax.numpy as jnp
from jax import lax
from jax.sharding import PartitionSpec as P

H = 16
HD = 72


EPS = 1e-06
CURVE = 0.7978845608028654
FLOOR = -1e30
HEAD_BLOCK = 4
QUERY_BLOCK = 512


def gelu_tanh(value):
    return 0.5 * value * (1.0 + jnp.tanh(CURVE * (value + 0.044715 * value * value * value)))


def normalize(value):
    centred = value - jnp.mean(value, axis=-1, keepdims=True)
    inverse = lax.rsqrt(jnp.mean(centred * centred, axis=-1, keepdims=True) + EPS)
    return (centred * inverse, inverse)


def norm_back(grad, normal, inverse):
    return inverse * (
        grad
        - jnp.mean(grad, axis=-1, keepdims=True)
        - normal * jnp.mean(grad * normal, axis=-1, keepdims=True)
    )


def cross(left, right):
    return lax.dot_general(
        left, right, (((0,), (0,)), ((), ())), preferred_element_type=jnp.float32
    )


def cross_exact(left, right):
    return lax.dot_general(
        left,
        right,
        (((0,), (0,)), ((), ())),
        precision=lax.Precision.HIGHEST,
        preferred_element_type=jnp.float32,
    )


def against(left, right):
    return lax.dot_general(
        left, right, (((1,), (1,)), ((), ())), preferred_element_type=jnp.float32
    )


def scores_of(query, keys, same):
    scaled = jnp.einsum("qhd,khd->hqk", query, keys, preferred_element_type=jnp.float32) * HD ** (
        -0.5
    )
    return jnp.where(same[None], scaled, FLOOR)


def per_crop(table, crop, slots):
    total = jnp.zeros((crop.shape[0], crop.shape[1], table.shape[2]), jnp.float32)
    for slot in range(slots):
        total = total + jnp.where(crop[:, :, None] == slot, table[:, slot : slot + 1, :], 0.0)
    return total


def crop_sums(block, crop, slots):
    return jnp.stack(
        [jnp.sum(jnp.where(crop[:, :, None] == slot, block, 0.0), axis=1) for slot in range(slots)],
        axis=1,
    )


def attend_row(packed, crop):
    pack = packed.shape[0]
    parts = packed.reshape(pack, 3, H, HD)
    span = min(QUERY_BLOCK, pack)
    band = min(HEAD_BLOCK, H)
    results = []
    sums = []
    for start in range(0, pack, span):
        same = crop[start : start + span, None] == crop[None, :]
        block_results = []
        block_sums = []
        for head in range(0, H, band):
            scores = scores_of(
                parts[start : start + span, 0, head : head + band],
                parts[:, 1, head : head + band],
                same,
            )
            top = jnp.max(scores, axis=2, keepdims=True)
            weights = jnp.exp(scores - top)
            total = jnp.sum(weights, axis=2, keepdims=True)
            probs = (weights / total).astype(jnp.bfloat16)
            block_results.append(
                jnp.einsum(
                    "hqk,khd->qhd",
                    probs,
                    parts[:, 2, head : head + band],
                    preferred_element_type=jnp.float32,
                )
            )
            block_sums.append(top + jnp.log(total))
        results.append(jnp.concatenate(block_results, axis=1))
        sums.append(jnp.concatenate(block_sums, axis=0))
    heads_out = jnp.concatenate(results, axis=0).reshape(pack, H * HD).astype(jnp.bfloat16)
    return (heads_out, jnp.concatenate(sums, axis=1))


def attend_row_back(packed, crop, sums, grad_heads):
    pack = packed.shape[0]
    parts = packed.reshape(pack, 3, H, HD)
    grad_parts = grad_heads.reshape(pack, H, HD)
    span = min(QUERY_BLOCK, pack)
    band = min(HEAD_BLOCK, H)
    scale = HD ** (-0.5)
    query_grads = []
    key_grads = []
    value_grads = []
    for head in range(0, H, band):
        keys = parts[:, 1, head : head + band]
        values = parts[:, 2, head : head + band]
        key_total = jnp.zeros((pack, band, HD), jnp.float32)
        value_total = jnp.zeros((pack, band, HD), jnp.float32)
        head_query = []
        for start in range(0, pack, span):
            same = crop[start : start + span, None] == crop[None, :]
            query = parts[start : start + span, 0, head : head + band]
            grad_block = grad_parts[start : start + span, head : head + band]
            scores = scores_of(query, keys, same)
            probs = jnp.exp(scores - sums[head : head + band, start : start + span])
            value_total = value_total + jnp.einsum(
                "hqk,qhd->khd",
                probs.astype(jnp.bfloat16),
                grad_block,
                preferred_element_type=jnp.float32,
            )
            grad_probs = jnp.einsum(
                "qhd,khd->hqk", grad_block, values, preferred_element_type=jnp.float32
            )
            inner = jnp.sum(probs * grad_probs, axis=2, keepdims=True)
            grad_scores = (probs * (grad_probs - inner)).astype(jnp.bfloat16)
            head_query.append(
                jnp.einsum("hqk,khd->qhd", grad_scores, keys, preferred_element_type=jnp.float32)
                * scale
            )
            key_total = (
                key_total
                + jnp.einsum("hqk,qhd->khd", grad_scores, query, preferred_element_type=jnp.float32)
                * scale
            )
        query_grads.append(jnp.concatenate(head_query, axis=0))
        key_grads.append(key_total)
        value_grads.append(value_total)
    stacked = jnp.stack(
        [
            jnp.concatenate(query_grads, axis=1),
            jnp.concatenate(key_grads, axis=1),
            jnp.concatenate(value_grads, axis=1),
        ],
        axis=1,
    )
    return stacked.reshape(pack, 3 * H * HD).astype(jnp.bfloat16)


def shards(
    tokens,
    lengths,
    condition,
    keep_mask,
    group_mask,
    qkv_weight,
    out_weight,
    mod_weight,
    out_bias,
    mod_bias,
    up_weight,
    up_bias,
    down_weight,
    down_bias,
    cotangent,
):
    rows, pack, width = tokens.shape
    slots = lengths.shape[1]
    groups = group_mask.shape[2]
    count = rows * pack
    qkv_full, out_full, mod_full, out_bias_full, mod_bias_full, up_bias_full, down_bias_full = (
        lax.all_gather(qkv_weight, ("row", "col"), axis=0, tiled=True),
        lax.all_gather(out_weight, ("row", "col"), axis=0, tiled=True),
        lax.all_gather(mod_weight, ("row", "col"), axis=0, tiled=True),
        lax.all_gather(out_bias, ("row", "col"), axis=0, tiled=True),
        lax.all_gather(mod_bias, ("row", "col"), axis=0, tiled=True),
        lax.all_gather(up_bias, ("row", "col"), axis=0, tiled=True),
        lax.all_gather(down_bias, ("row", "col"), axis=0, tiled=True),
    )
    up_half, down_half = (
        lax.all_gather(up_weight, "col", axis=1, tiled=True),
        lax.all_gather(down_weight, "col", axis=0, tiled=True),
    )
    up_full, down_full = (
        lax.all_gather(up_half, "row", axis=0, tiled=True),
        lax.all_gather(down_half, "row", axis=1, tiled=True),
    )
    hidden_units = up_full.shape[1]
    group_width = hidden_units // groups
    ends = jnp.cumsum(lengths, axis=1)
    places = jnp.arange(pack, dtype=jnp.int32)
    crop = jnp.sum((places[None, :, None] >= ends[:, None, :]).astype(jnp.int32), axis=2)
    valid = (crop < slots).astype(jnp.float32).reshape(count, 1)
    keeps = keep_mask.reshape(count, 1).astype(jnp.float32)
    silu_cond = (
        jax.nn.silu(condition.astype(jnp.float32)).astype(jnp.bfloat16).reshape(rows * slots, width)
    )
    mods = jnp.dot(silu_cond, mod_full, preferred_element_type=jnp.float32) + mod_bias_full.astype(
        jnp.float32
    )
    mods = mods.reshape(rows, slots, 6 * width)
    per_token = per_crop(mods, crop, slots).reshape(count, 6 * width)
    shift_one, scale_one, gate_one, shift_two, scale_two, gate_two = jnp.split(per_token, 6, axis=1)
    channel = per_crop(group_mask.astype(jnp.float32), crop, slots).reshape(count, groups, 1)
    inputs = tokens.reshape(count, width).astype(jnp.float32)
    normal_one, inverse_one = normalize(inputs)
    first_in = (normal_one * (1.0 + scale_one) + shift_one).astype(jnp.bfloat16)
    projected = jnp.dot(first_in, qkv_full, preferred_element_type=jnp.float32).astype(jnp.bfloat16)
    packed_rows = projected.reshape(rows, pack, 3 * width)
    heads_rows, sums_rows = lax.map(lambda item: attend_row(item[0], item[1]), (packed_rows, crop))
    heads_out = heads_rows.reshape(count, width)
    attn = jnp.dot(heads_out, out_full, preferred_element_type=jnp.float32) + out_bias_full.astype(
        jnp.float32
    )
    resid = inputs + gate_one * attn
    normal_two, inverse_two = normalize(resid)
    second_in = (normal_two * (1.0 + scale_two) + shift_two).astype(jnp.bfloat16)
    pre = jnp.dot(second_in, up_full, preferred_element_type=jnp.float32) + up_bias_full.astype(
        jnp.float32
    )
    activated, gelu_pullback = jax.vjp(gelu_tanh, pre)
    hidden = (
        (activated.reshape(count, groups, group_width) * channel)
        .reshape(count, hidden_units)
        .astype(jnp.bfloat16)
    )
    mlp_out = jnp.dot(
        hidden, down_full, preferred_element_type=jnp.float32
    ) + down_bias_full.astype(jnp.float32)
    final = resid + keeps * gate_two * mlp_out
    block_out = (valid * final).astype(jnp.bfloat16).reshape(rows, pack, width)
    qkv_back, out_back = (
        lax.all_gather(qkv_weight, ("row", "col"), axis=0, tiled=True),
        lax.all_gather(out_weight, ("row", "col"), axis=0, tiled=True),
    )
    up_part, down_part = (
        lax.all_gather(up_weight, "col", axis=1, tiled=True),
        lax.all_gather(down_weight, "col", axis=0, tiled=True),
    )
    up_back, down_back = (
        lax.all_gather(up_part, "row", axis=0, tiled=True),
        lax.all_gather(down_part, "row", axis=1, tiled=True),
    )
    grad_final = valid * cotangent.reshape(count, width).astype(jnp.float32)
    grad_mlp = (keeps * gate_two * grad_final).astype(jnp.bfloat16)
    grad_gate_two = keeps * grad_final * mlp_out
    grad_down = cross(hidden, grad_mlp)
    grad_downbias = jnp.sum(grad_mlp.astype(jnp.float32), axis=0)
    grad_hidden = against(grad_mlp, down_back)
    grad_masked = (grad_hidden.reshape(count, groups, group_width) * channel).reshape(
        count, hidden_units
    )
    grad_pre = gelu_pullback(grad_masked)[0].astype(jnp.bfloat16)
    grad_up = cross(second_in, grad_pre)
    grad_upbias = jnp.sum(grad_pre.astype(jnp.float32), axis=0)
    grad_second = against(grad_pre, up_back)
    grad_resid = grad_final + norm_back(grad_second * (1.0 + scale_two), normal_two, inverse_two)
    grad_attn = (gate_one * grad_resid).astype(jnp.bfloat16)
    grad_gate_one = grad_resid * attn
    grad_out = cross(heads_out, grad_attn)
    grad_outbias = jnp.sum(grad_attn.astype(jnp.float32), axis=0)
    grad_heads = against(grad_attn, out_back).astype(jnp.bfloat16).reshape(rows, pack, width)
    grad_up_rows, grad_down_rows = (
        lax.psum_scatter(
            grad_up.astype(jnp.bfloat16), "row", scatter_dimension=0, tiled=True
        ).astype(jnp.float32),
        lax.psum_scatter(
            grad_down.astype(jnp.bfloat16), "row", scatter_dimension=1, tiled=True
        ).astype(jnp.float32),
    )
    grad_up_shard, grad_down_shard = (
        lax.psum_scatter(grad_up_rows, "col", scatter_dimension=1, tiled=True),
        lax.psum_scatter(grad_down_rows, "col", scatter_dimension=0, tiled=True),
    )
    grad_projected = lax.map(
        lambda item: attend_row_back(item[0], item[1], item[2], item[3]),
        (packed_rows, crop, sums_rows, grad_heads),
    )
    grad_projected = grad_projected.reshape(count, 3 * width)
    grad_qkv = cross(first_in, grad_projected)
    grad_first = against(grad_projected, qkv_back)
    grad_tokens = grad_resid + norm_back(grad_first * (1.0 + scale_one), normal_one, inverse_one)
    grad_blocks = [
        grad_first,
        grad_first * normal_one,
        grad_gate_one,
        grad_second,
        grad_second * normal_two,
        grad_gate_two,
    ]
    grad_mods = jnp.concatenate(
        [crop_sums(block.reshape(rows, pack, width), crop, slots) for block in grad_blocks], axis=2
    )
    grad_mods = grad_mods.reshape(rows * slots, 6 * width)
    cond_values = silu_cond.astype(jnp.float32)
    half_qkv, half_out, half_outbias, half_upbias, half_downbias = (
        lax.psum_scatter(
            grad_qkv.astype(jnp.bfloat16), "row", scatter_dimension=0, tiled=True
        ).astype(jnp.float32),
        lax.psum_scatter(
            grad_out.astype(jnp.bfloat16), "row", scatter_dimension=0, tiled=True
        ).astype(jnp.float32),
        lax.psum_scatter(
            grad_outbias.astype(jnp.bfloat16), "row", scatter_dimension=0, tiled=True
        ).astype(jnp.float32),
        lax.psum_scatter(
            grad_upbias.astype(jnp.bfloat16), "row", scatter_dimension=0, tiled=True
        ).astype(jnp.float32),
        lax.psum_scatter(
            grad_downbias.astype(jnp.bfloat16), "row", scatter_dimension=0, tiled=True
        ).astype(jnp.float32),
    )
    grad_qkv_shard, grad_out_shard, grad_outbias_shard, grad_upbias_shard, grad_downbias_shard = (
        lax.psum_scatter(half_qkv, "col", scatter_dimension=0, tiled=True),
        lax.psum_scatter(half_out, "col", scatter_dimension=0, tiled=True),
        lax.psum_scatter(half_outbias, "col", scatter_dimension=0, tiled=True),
        lax.psum_scatter(half_upbias, "col", scatter_dimension=0, tiled=True),
        lax.psum_scatter(half_downbias, "col", scatter_dimension=0, tiled=True),
    )
    all_cond, all_grad_mods = (
        lax.all_gather(cond_values.astype(jnp.bfloat16), ("row", "col"), axis=0, tiled=True).astype(
            cond_values.dtype
        ),
        lax.all_gather(grad_mods.astype(jnp.bfloat16), ("row", "col"), axis=0, tiled=True).astype(
            grad_mods.dtype
        ),
    )
    devices = lax.axis_size(("row", "col"))
    position = lax.axis_index(("row", "col"))
    share = width // devices
    mod_share = 6 * width // devices
    cond_columns = lax.dynamic_slice_in_dim(all_cond, position * share, share, 1)
    grad_mod_shard = cross_exact(cond_columns, all_grad_mods)
    grad_modbias_shard = jnp.sum(
        lax.dynamic_slice_in_dim(all_grad_mods, position * mod_share, mod_share, 1), axis=0
    )
    return (
        block_out,
        grad_tokens.reshape(rows, pack, width),
        grad_qkv_shard,
        grad_out_shard,
        grad_mod_shard,
        grad_outbias_shard,
        grad_modbias_shard,
        grad_up_shard,
        grad_upbias_shard,
        grad_down_shard,
        grad_downbias_shard,
    )


def solution(mesh):
    placed = (
        P(("row", "col"), None, None),
        P(("row", "col"), None),
        P(("row", "col"), None, None),
        P(("row", "col"), None),
        P(("row", "col"), None, None),
        P(("row", "col"), None),
        P(("row", "col"), None),
        P(("row", "col"), None),
        P(("row", "col")),
        P(("row", "col")),
        P("row", "col"),
        P(("row", "col")),
        P("col", "row"),
        P(("row", "col")),
        P(("row", "col"), None, None),
    )
    return jax.shard_map(
        shards,
        mesh=mesh,
        in_specs=placed,
        out_specs=(
            P(("row", "col"), None, None),
            P(("row", "col"), None, None),
            P(("row", "col"), None),
            P(("row", "col"), None),
            P(("row", "col"), None),
            P(("row", "col")),
            P(("row", "col")),
            P("row", "col"),
            P(("row", "col")),
            P("col", "row"),
            P(("row", "col")),
        ),
        check_vma=False,
    )
```

profile of v0, /device:TPU:19, one launch (start us, length us, event | category | flops | bytes accessed | tf_op | source)
XLA Modules:
  0.0 1469.5 jit_solution(8650699768787540910)
XLA Ops:
  10.7 59.5 %all-gather.14.cloned.1.call-done = bf16[576,4608]{0,1:T(8,128)(2,1)} async-done(((bf16[576,288]{0,1:T(8,128)(2,1)}), bf16[576,4608]{0,1:T(8,128)(2,1)}) %all-gather.14.cloned.1.call-update) | async-done | bytes 5308432 | tf_op jit(solution)/shard_map/all_gather | solution.py:201
  70.2 8.2 copy.89
  80.1 39.9 %all-reduce.15 = (bf16[6912]{0:T(1024)(128)(2,1)S(1)}, bf16[1152]{0:T(1024)(128)(2,1)S(1)}, bf16[4608]{0:T(1024)(128)(2,1)S(1)}, bf16[1152]{0:T(1024)(128)(2,1)}) all-reduce(bf16[6912]{0:T(1024)(128)(2,1)S(1)} %dynamic-update-slice, bf16[1152]{0:T(1024)(128)(2,1)S(1)} %dynamic-update-slice.1, ...), channel_id=1, replica_groups=mesh['row'=2,'col'=16] {'row','col'}, use_global_device_ids=true, to_apply=%add | all-reduce | flops 13824 | bytes 55296
  122.2 8.9 mul.441
  131.1 18.9 %copy.90 = f32[1024,4608]{1,0:T(8,128)} copy(f32[1024,4608]{0,1:T(8,128)} %bitcast.346) | data formatting | bytes 37748736 | tf_op jit(solution)/shard_map/mul | solution.py:243
  157.1 34.5 %all-gather.18.cloned.1.call-done = bf16[4608,576]{1,0:T(8,128)(2,1)} async-done(((bf16[288,576]{1,0:T(8,128)(2,1)}), bf16[4608,576]{1,0:T(8,128)(2,1)}) %all-gather.18.cloned.1.call-update) | async-done | bytes 5308432 | tf_op jit(solution)/shard_map/all_gather | solution.py:202
  191.6 8.2 copy.91
  199.9 73.2 %all-gather.26.cloned.1.call-done = bf16[32,36,3456]{2,1,0:T(8,128)(2,1)} async-done(((bf16[1,36,3456]{2,1,0:T(8,128)(2,1)}), bf16[32,36,3456]{2,1,0:T(8,128)(2,1)}) %all-gather.26.cloned.1.call-update) | async-done | bytes 7962640 | tf_op jit(solution)/shard_map/all_gather | solution.py:192
  273.1 12.5 reshape.624
  285.6 107.7 %all-gather.24.cloned.1.call-done = bf16[32,36,6912]{2,1,0:T(8,128)(2,1)} async-done(((bf16[1,36,6912]{2,1,0:T(8,128)(2,1)}), bf16[32,36,6912]{2,1,0:T(8,128)(2,1)}) %all-gather.24.cloned.1.call-update) | async-done | bytes 15925264 | tf_op jit(solution)/shard_map/all_gather | solution.py:194
  393.3 19.4 %reshape.622 = bf16[1152,6912]{1,0:T(8,128)(2,1)} reshape(bf16[32,36,6912]{2,1,0:T(8,128)(2,1)} %all-gather.24.cloned.1.call-done) | data formatting | bytes 31850496
  412.7 8.5 fusion.8
  421.5 33.1 %select_add_fusion = f32[1024,6912]{1,0:T(8,128)} fusion(f32[6912]{0:T(1024)S(1)} %get-tuple-element.135, f32[6912]{0:T(1024)S(1)} %get-tuple-element.136, f32[6912]{0:T(1024)S(1)} %get-tuple-element.134, pred[1024]{0:T(1024)(128)(4,1)S(1)} %get-tuple-element.169, pred[1024]{0:T(1024)(128)(4,1)S(1)} %get-tuple-element.170, ...), kind=kLoop, calls=%fused_computation | loop fusion | flops 35389440 | bytes 28397568 | tf_op jit(solution)/shard_map/add | solution.py:67
  460.6 14.8 %convolution_convert_fusion.4 = bf16[1024,3456]{1,0:T(8,128)(2,1)} fusion(bf16[1024,1152]{1,0:T(8,128)(2,1)S(1)} %fusion.34, bf16[1152,3456]{1,0:T(8,128)(2,1)} %reshape.624), kind=kOutput, calls=%fused_computation.66 | convolution fusion | flops 8157265920 | bytes 17399808 | tf_op jit(solution)/shard_map/dot_general | solution.py:228
  475.4 10.3 copy.88
  506.1 6.9 fusion.213
  512.9 6.6 fusion.214
  578.4 9.8 fusion.204
  596.2 27.6 %multiply_convert_fusion = (bf16[1024,4608]{1,0:T(8,128)(2,1)}, f32[1024,4608]{1,0:T(8,128)}) fusion(f32[1024,4608]{1,0:T(8,128)} %copy.90, f32[4608]{0:T(1024)S(1)} %copy-done.79, bf16[1024,1152]{1,0:T(8,128)(2,1)} %fusion.41, bf16[1152,4608]{1,0:T(8,128)(2,1)} %all-gather.16.cloned.1.call-done), kind=kOutput, calls=%fused_computation.13 | convolution fusion | flops 10923540480 | bytes 60180480 | tf_op jit(solution)/shard_map/dot_general | solution.py:238
  623.7 17.2 %convolution_convert_fusion = bf16[4608,1152]{0,1:T(8,128)(2,1)} fusion(bf16[1024,4608]{1,0:T(8,128)(2,1)} %get-tuple-element.198, bf16[1024,1152]{1,0:T(8,128)(2,1)S(1)} %copy-done.32), kind=kOutput, calls=%fused_computation.5 | convolution fusion | flops 10876944384 | bytes 22413312 | tf_op jit(solution)/shard_map/dot_general | solution.py:36
  641.6 15.3 %all-gather.20.cloned.1.call-done = bf16[4608,1152]{0,1:T(8,128)(2,1)} async-done(((bf16[4608,576]{0,1:T(8,128)(2,1)}), bf16[4608,1152]{0,1:T(8,128)(2,1)}) %all-gather.20.cloned.1.call-update) | async-done | bytes 10616848 | tf_op jit(solution)/shard_map/all_gather | solution.py:206
  656.9 34.1 %fusion.216 = (bf16[4608]{0:T(1024)(128)(2,1)}, bf16[1024,4608]{1,0:T(8,128)(2,1)}) fusion(f32[1024,4608]{1,0:T(8,128)} %copy.90, bf16[1024,1152]{1,0:T(8,128)(2,1)S(1)} %copy-done.32, bf16[4608,1152]{0,1:T(8,128)(2,1)} %all-gather.20.cloned.1.call-done, f32[1024,4608]{1,0:T(8,128)} %get-tuple-element.199, f32[4608]{0:T(1024)S(1)} %copy-done.79), kind=kOutput, calls=%fused_computation.350 | convolution fusion | flops 10999033856 | bytes 60189696 | tf_op jit(solution)/shard_map/dot_general | solution.py:52
  691.1 17.1 %convolution_convert_fusion.1 = bf16[1152,4608]{1,0:T(8,128)(2,1)} fusion(bf16[1024,1152]{1,0:T(8,128)(2,1)S(1)} %copy-done.27, bf16[1024,4608]{1,0:T(8,128)(2,1)} %get-tuple-element.220), kind=kOutput, calls=%fused_computation.6 | convolution fusion | flops 10876944384 | bytes 22413312 | tf_op jit(solution)/shard_map/dot_general | solution.py:36
  708.3 20.8 %fusion.81 = (f32[1024,1152]{1,0:T(8,128)}, f32[1024,1152]{1,0:T(8,128)}) fusion(f32[1024,1152]{1,0:T(8,128)} %copy-done.11, f32[1024]{0:T(1024)S(1)} %add_rsqrt_fusion, f32[1024]{0:T(1024)S(1)} %broadcast_multiply_fusion.4, bf16[1024,4608]{1,0:T(8,128)(2,1)} %get-tuple-element.220, bf16[1152,4608]{1,0:T(8,128)(2,1)} %all-gather.16.cloned.1.call-done), kind=kOutput, calls=%fused_computation.165 | convolution fusion | flops 10875174912 | bytes 34217984 | tf_op jit(solution)/shard_map/dot_general | solution.py:52
  729.2 26.3 %select_reduce_fusion.8 = (bf16[1152]{0:T(1024)(128)(2,1)}, bf16[1152]{0:T(1024)(128)(2,1)}, bf16[1152]{0:T(1024)(128)(2,1)}, f32[1024]{0:T(1024)S(1)}, f32[1024...) fusion(f32[1024,1152]{1,0:T(8,128)} %get-tuple-element.201, ...), kind=kOutput, calls=%fused_computation.122 | convolution fusion | flops 10912912384 | bytes 48418560 | tf_op jit(solution)/shard_map/dot_general | solution.py:247
  755.5 10.8 fusion.202
  836.3 7.2 multiply_reduce_fusion.7
  843.6 7.3 multiply_convert_fusion.8
  869.7 6.2 fusion.119
  891.5 6.7 multiply_reduce_fusion.2
  898.3 6.6 multiply_reduce_fusion.4
  904.9 6.8 multiply_reduce_fusion.6
  916.3 7.2 multiply_convert_fusion.3
  926.4 6.9 multiply_convert_fusion.5
  957.5 10.9 convolution_convert_fusion.2
  970.1 25.9 %fusion.198 = (f32[1024]{0:T(1024)S(1)}, f32[1024]{0:T(1024)S(1)}, bf16[1152]{0:T(1024)(128)(2,1)S(1)}, bf16[1152]{0:T(1024)(128)(2,1)S(1)}, bf16[1152]{0:T(1024...) fusion(f32[1024,6912]{1,0:T(8,128)} %select_add_fusion, ...), kind=kOutput, calls=%fused_computation.336 | convolution fusion | flops 8186745856 | bytes 36314368 | tf_op jit(solution)/shard_map/dot_general | solution.py:52
  997.0 8.9 copy.99
  1006.0 8.8 copy.97
  1019.3 35.2 %all-gather = bf16[1,96,1152]{2,0,1:T(2,128)(2,1)S(1)} all-gather(bf16[1,3,1152]{2,0,1:T(2,128)(2,1)S(1)} %copy-done.39), channel_id=2, replica_groups=mesh['row'=2,'col'=16] {'row','col'}, dimensions={1}, use_global_device_ids=true | all-gather | bytes 228096 | tf_op jit(solution)/shard_map/all_gather | solution.py:341
  1069.5 185.0 %fusion.199 = (f32[48,3456]{1,0:T(8,128)S(1)}, f32[48,1152]{1,0:T(8,128)S(1)}) fusion(f32[576,3456]{1,0:T(8,128)} %convert_element_type.297, f32[576,1152]{1,0:T(8,128)} %convert_element_type.299), kind=kCustom, calls=%all-reduce-scatter.2 | all-reduce-scatter fusion | flops 3538945 | bytes 11502080
  1257.2 8.3 fusion.39
  1265.5 6.3 all-reduce.16
  1286.1 101.5 %all-reduce.14 = (f32[576]{0:T(1024)S(1)}, f32[2304]{0:T(1024)S(1)}, f32[576]{0:T(1024)S(1)}) all-reduce(f32[576]{0:T(1024)S(1)} %dynamic-slice_convert_fusion.2, f32[2304]{0:T(1024)S(1)} %dynamic-slice_convert_fusion, f32[576]{0:T(1024)S(1)} %dynamic-slice_convert_fusion.1), channel_id=9, replica_groups=mesh['row'=2,'col'=16] {'col'}, use_global_device_ids=true, to_apply=%region_58.59.clone | all-reduce | flops 3456 | bytes 27648
  1392.1 7.2 collective-permute-start.4
  1402.5 10.9 collective-permute-done.4
  1417.6 6.5 collective-permute-done.3
  1424.1 19.0 %concatenate.71 = f32[228,3456]{1,0:T(8,128)} concatenate(f32[36,3456]{1,0:T(8,128)} %collective-permute-done.3, f32[48,3456]{1,0:T(8,128)S(1)} %collective-permute-done.2, f32[48,3456]{1,0:T(8,128)} %collective-permute-done.1, f32[48,3456]{1,0:T(8,128)} %collective-permute-done, f32[48,3456]{1,0:T(8,128)S(1)} %get-tuple-element.158), dimensions={0} | concatenate | bytes 6303744
  1445.0 17.7 %reduce-scatter.23.cloned.1.call-done = f32[288,576]{1,0:T(8,128)} async-done(((f32[4608,576]{1,0:T(8,128)}), f32[288,576]{1,0:T(8,128)}) %reduce-scatter.23.cloned.1.call-update) | async-done | bytes 663568
  (505 shorter events, 293.0 us)
Async XLA Ops:
  7.2 63.0 %all-gather.14.cloned.1.call-start = ((), (), s32[]{:S(2)}) async-start(), calls=%async_computation.6 | async-start | bytes 6266880 | tf_op jit(solution)/shard_map/all_gather | solution.py:201
  7.9 144.1 %all-gather.28.cloned.1.call-start = ((), (), s32[]{:S(2)}) async-start(), calls=%async_computation.17 | async-start | bytes 3041280 | tf_op jit(solution)/shard_map/all_gather | solution.py:193
  8.7 183.0 %all-gather.18.cloned.1.call-start = ((), (), s32[]{:S(2)}) async-start(), calls=%async_computation.8 | async-start | bytes 6266880 | tf_op jit(solution)/shard_map/all_gather | solution.py:202
  9.4 263.7 %all-gather.26.cloned.1.call-start = ((), (), s32[]{:S(2)}) async-start(), calls=%async_computation.16 | async-start | bytes 9123840 | tf_op jit(solution)/shard_map/all_gather | solution.py:192
  10.0 383.3 %all-gather.24.cloned.1.call-start = ((), (), s32[]{:S(2)}) async-start(), calls=%async_computation.15 | async-start | bytes 18247680 | tf_op jit(solution)/shard_map/all_gather | solution.py:194
  10.6 67.9 %copy-start.108 = (s32[1,3,16]{2,0,1:T(1,128)S(1)}, s32[1,3,16]{2,0,1:T(1,128)}, u32[]{:S(2)}) copy-start(s32[1,3,16]{2,0,1:T(1,128)} %param.19) | copy-start | bytes 580
  10.6 67.9 %copy-start.97 = (s32[1,1024]{1,0:T(1,128)S(1)}, s32[1,1024]{1,0:T(1,128)}, u32[]{:S(2)}) copy-start(s32[1,1024]{1,0:T(1,128)} %param.18) | copy-start | bytes 12292
  10.6 68.5 %copy-start.109 = (bf16[36]{0:T(256)(128)(2,1)S(1)}, bf16[36]{0:T(256)(128)(2,1)}, u32[]{:S(2)}) copy-start(bf16[36]{0:T(256)(128)(2,1)} %param.23) | copy-start | bytes 220
  10.6 68.7 %copy-start.110 = (bf16[36]{0:T(256)(128)(2,1)S(1)}, bf16[36]{0:T(256)(128)(2,1)}, u32[]{:S(2)}) copy-start(bf16[36]{0:T(256)(128)(2,1)} %param.28) | copy-start | bytes 220
  10.6 69.0 %copy-start.111 = (bf16[144]{0:T(256)(128)(2,1)S(1)}, bf16[144]{0:T(256)(128)(2,1)}, u32[]{:S(2)}) copy-start(bf16[144]{0:T(256)(128)(2,1)} %param.26) | copy-start | bytes 868
  10.6 69.2 %copy-start.112 = (bf16[216]{0:T(256)(128)(2,1)S(1)}, bf16[216]{0:T(256)(128)(2,1)}, u32[]{:S(2)}) copy-start(bf16[216]{0:T(256)(128)(2,1)} %param.24) | copy-start | bytes 1300
  10.6 110.6 %copy-start.113 = (s32[1,3]{1,0:T(1,128)S(1)}, s32[1,3]{1,0:T(1,128)}, u32[]{:S(2)}) copy-start(s32[1,3]{1,0:T(1,128)} %param.16) | copy-start | bytes 40
  10.6 585.6 %all-gather.16.cloned.1.call-start = ((), (), s32[]{:S(2)}) async-start(), calls=%async_computation.7 | async-start | bytes 15925248 | tf_op jit(solution)/shard_map/all_gather | solution.py:205
  78.4 578.5 %all-gather.20.cloned.1.call-start = ((), (), s32[]{:S(2)}) async-start(), calls=%async_computation.9 | async-start | bytes 15925248 | tf_op jit(solution)/shard_map/all_gather | solution.py:206
  122.1 299.3 %copy-start.85 = (pred[1024]{0:T(1024)(128)(4,1)}, pred[1024]{0:T(1024)(128)(4,1)S(1)}, u32[]{:S(2)}) copy-start(pred[1024]{0:T(1024)(128)(4,1)S(1)} %get-tuple-element.169) | copy-start | bytes 3076
  122.1 299.3 %copy-start.88 = (pred[1024]{0:T(1024)(128)(4,1)}, pred[1024]{0:T(1024)(128)(4,1)S(1)}, u32[]{:S(2)}) copy-start(pred[1024]{0:T(1024)(128)(4,1)S(1)} %get-tuple-element.170) | copy-start | bytes 3076
  122.1 299.4 %copy-start.91 = (pred[1024]{0:T(1024)(128)(4,1)}, pred[1024]{0:T(1024)(128)(4,1)S(1)}, u32[]{:S(2)}) copy-start(pred[1024]{0:T(1024)(128)(4,1)S(1)} %get-tuple-element.171) | copy-start | bytes 3076
  150.4 304.2 %copy-start.41 = (f32[1024]{0:T(1024)}, f32[1024]{0:T(1024)S(1)}, u32[]{:S(2)}) copy-start(f32[1024]{0:T(1024)S(1)} %broadcast_multiply_fusion.5) | copy-start | bytes 12292
  151.2 303.4 %copy-start.45 = (f32[1024]{0:T(1024)}, f32[1024]{0:T(1024)S(1)}, u32[]{:S(2)}) copy-start(f32[1024]{0:T(1024)S(1)} %add_rsqrt_fusion.1) | copy-start | bytes 12292
  151.9 260.8 %copy-start.38 = (bf16[1,3,1152]{2,0,1:T(2,128)(2,1)}, bf16[1,3,1152]{2,0,1:T(2,128)(2,1)S(1)}, u32[]{:S(2)}) copy-start(bf16[1,3,1152]{2,0,1:T(2,128)(2,1)S(1)} %fusion.191) | copy-start | bytes 20740
  199.8 797.2 %reduce-scatter.21.cloned.1.call-start = ((), (), s32[]{:S(2)}) async-start(), calls=%async_computation.13 | async-start | bytes 15925248 | tf_op jit(solution)/shard_map/reduce_scatter | solution.py:287
  491.8 38.2 %copy-start.47 = (f32[4,512]{1,0:T(4,128)}, f32[4,512]{1,0:T(4,128)S(1)}, u32[]{:S(2)}) copy-start(f32[4,512]{1,0:T(4,128)S(1)} %get-tuple-element.181) | copy-start | bytes 24580
  494.9 42.9 %copy-start.2 = (f32[4,512,1024]{2,1,0:T(8,128)}, f32[4,512,1024]{2,1,0:T(8,128)S(1)}, u32[]{:S(2)}) copy-start(f32[4,512,1024]{2,1,0:T(8,128)S(1)} %get-tuple-element.184) | copy-start | bytes 25165828
  494.9 42.9 %copy-start.49 = (f32[4,512]{1,0:T(4,128)}, f32[4,512]{1,0:T(4,128)S(1)}, u32[]{:S(2)}) copy-start(f32[4,512]{1,0:T(4,128)S(1)} %get-tuple-element.183) | copy-start | bytes 24580
  498.6 44.2 %copy-start.1 = (f32[4,512,1024]{2,1,0:T(8,128)}, f32[4,512,1024]{2,1,0:T(8,128)S(1)}, u32[]{:S(2)}) copy-start(f32[4,512,1024]{2,1,0:T(8,128)S(1)} %get-tuple-element.186) | copy-start | bytes 25165828
  498.6 44.2 %copy-start.51 = (f32[4,512]{1,0:T(4,128)}, f32[4,512]{1,0:T(4,128)S(1)}, u32[]{:S(2)}) copy-start(f32[4,512]{1,0:T(4,128)S(1)} %get-tuple-element.185) | copy-start | bytes 24580
  502.3 45.5 %copy-start = (f32[4,512,1024]{2,1,0:T(8,128)}, f32[4,512,1024]{2,1,0:T(8,128)S(1)}, u32[]{:S(2)}) copy-start(f32[4,512,1024]{2,1,0:T(8,128)S(1)} %get-tuple-element.188) | copy-start | bytes 25165828
  502.3 45.5 %copy-start.53 = (f32[4,512]{1,0:T(4,128)}, f32[4,512]{1,0:T(4,128)S(1)}, u32[]{:S(2)}) copy-start(f32[4,512]{1,0:T(4,128)S(1)} %get-tuple-element.187) | copy-start | bytes 24580
  506.0 46.7 %copy-start.3 = (f32[4,512,1024]{2,1,0:T(8,128)}, f32[4,512,1024]{2,1,0:T(8,128)S(1)}, u32[]{:S(2)}) copy-start(f32[4,512,1024]{2,1,0:T(8,128)S(1)} %get-tuple-element.190) | copy-start | bytes 25165828
  506.1 46.7 %copy-start.55 = (f32[4,512]{1,0:T(4,128)}, f32[4,512]{1,0:T(4,128)S(1)}, u32[]{:S(2)}) copy-start(f32[4,512]{1,0:T(4,128)S(1)} %get-tuple-element.189) | copy-start | bytes 24580
  512.9 44.9 %copy-start.57 = (f32[4,512]{1,0:T(4,128)}, f32[4,512]{1,0:T(4,128)S(1)}, u32[]{:S(2)}) copy-start(f32[4,512]{1,0:T(4,128)S(1)} %get-tuple-element.191) | copy-start | bytes 24580
  519.5 43.4 %copy-start.59 = (f32[4,512]{1,0:T(4,128)}, f32[4,512]{1,0:T(4,128)S(1)}, u32[]{:S(2)}) copy-start(f32[4,512]{1,0:T(4,128)S(1)} %get-tuple-element.193) | copy-start | bytes 24580
  525.6 42.3 %copy-start.61 = (f32[4,512]{1,0:T(4,128)}, f32[4,512]{1,0:T(4,128)S(1)}, u32[]{:S(2)}) copy-start(f32[4,512]{1,0:T(4,128)S(1)} %get-tuple-element.195) | copy-start | bytes 24580
  640.9 365.0 %reduce-scatter.19.cloned.1.call-start = ((), (), s32[]{:S(2)}) async-start(), calls=%async_computation.12 | async-start | bytes 15925248 | tf_op jit(solution)/shard_map/reduce_scatter | solution.py:284
  656.9 34.1 %copy-start.27 = (bf16[1024,1152]{1,0:T(8,128)(2,1)S(1)}, bf16[1024,1152]{1,0:T(8,128)(2,1)}, u32[]{:S(2)}) copy-start(bf16[1024,1152]{1,0:T(8,128)(2,1)} %fusion.41) | copy-start | bytes 7077892
  708.2 347.1 %reduce-scatter.17.cloned.1.call-start = ((), (), s32[]{:S(2)}) async-start(), calls=%async_computation.11 | async-start | bytes 3981312 | tf_op jit(solution)/shard_map/reduce_scatter | solution.py:320
  916.3 147.4 %reduce-scatter.15.cloned.1.call-start = ((), (), s32[]{:S(2)}) async-start(), calls=%async_computation.10 | async-start | bytes 11943936 | tf_op jit(solution)/shard_map/reduce_scatter | solution.py:317
  968.5 420.9 %all-gather.22.cloned.1.call-start = ((), (), s32[]{:S(2)}) async-start(), calls=%async_computation.14 | async-start | bytes 2737152 | tf_op jit(solution)/shard_map/all_gather | solution.py:344
  997.0 448.1 %reduce-scatter.25.cloned.1.call-start = ((), (), s32[]{:S(2)}) async-start(), calls=%async_computation.19 | async-start | bytes 12533760
  1005.9 456.8 %reduce-scatter.23.cloned.1.call-start = ((), (), s32[]{:S(2)}) async-start(), calls=%async_computation.18 | async-start | bytes 12533760
  1255.3 27.9 %collective-permute-start.7 = (f32[36,1152]{1,0:T(8,128)}, f32[36,1152]{1,0:T(8,128)}, u32[]{:S(2)}, u32[]{:S(2)}) collective-permute-start(f32[36,1152]{1,0:T(8,128)} %slice.263), channel_id=1, source_target_pairs={{0,4},{1,5},{2,6},{3,7},{4,8},{5,9},{6,10},{7,11},{8,12},{9,13},{1... | collective-permute-start | bytes 497672
  1271.9 120.2 %collective-permute-start.6 = (f32[48,1152]{1,0:T(8,128)S(1)}, f32[48,1152]{1,0:T(8,128)S(1)}, u32[]{:S(2)}, u32[]{:S(2)}) collective-permute-start(f32[48,1152]{1,0:T(8,128)S(1)} %get-tuple-element.159), channel_id=1, source_target_pairs={{0,3},{1,4},{2,5},{3,6},{4,7},{5,8},{6,9},{7,10},{8,11},{9,12},{10... | collective-permute-start | bytes 663560
  1277.3 121.9 %collective-permute-start.5 = (f32[48,1152]{1,0:T(8,128)S(1)}, f32[48,1152]{1,0:T(8,128)S(1)}, u32[]{:S(2)}, u32[]{:S(2)}) collective-permute-start(f32[48,1152]{1,0:T(8,128)S(1)} %get-tuple-element.159), channel_id=1, source_target_pairs={{0,2},{1,3},{2,4},{3,5},{4,6},{5,7},{6,8},{7,9},{8,10},{9,11},{10,... | collective-permute-start | bytes 663560
  1279.3 144.8 %collective-permute-start.2 = (f32[48,3456]{1,0:T(8,128)S(1)}, f32[48,3456]{1,0:T(8,128)S(1)}, u32[]{:S(2)}, u32[]{:S(2)}) collective-permute-start(f32[48,3456]{1,0:T(8,128)S(1)} %get-tuple-element.158), channel_id=1, source_target_pairs={{0,3},{1,4},{2,5},{3,6},{4,7},{5,8},{6,9},{7,10},{8,11},{9,12},{10... | collective-permute-start | bytes 1990664
  1281.2 142.9 %collective-permute-start.1 = (f32[48,3456]{1,0:T(8,128)S(1)}, f32[48,3456]{1,0:T(8,128)}, u32[]{:S(2)}, u32[]{:S(2)}) collective-permute-start(f32[48,3456]{1,0:T(8,128)S(1)} %get-tuple-element.158), channel_id=1, source_target_pairs={{0,2},{1,3},{2,4},{3,5},{4,6},{5,7},{6,8},{7,9},{8,10},{9,11},{10,... | collective-permute-start | bytes 1990664
  1283.1 141.0 %collective-permute-start = (f32[48,3456]{1,0:T(8,128)S(1)}, f32[48,3456]{1,0:T(8,128)}, u32[]{:S(2)}, u32[]{:S(2)}) collective-permute-start(f32[48,3456]{1,0:T(8,128)S(1)} %get-tuple-element.158), channel_id=1, source_target_pairs={{0,1},{1,2},{2,3},{3,4},{4,5},{5,6},{6,7},{7,8},{8,9},{9,10},{10,1... | collective-permute-start | bytes 1990664
  1392.1 21.3 %collective-permute-start.4 = (f32[48,1152]{1,0:T(8,128)S(1)}, f32[48,1152]{1,0:T(8,128)}, u32[]{:S(2)}, u32[]{:S(2)}) collective-permute-start(f32[48,1152]{1,0:T(8,128)S(1)} %get-tuple-element.159), channel_id=1, source_target_pairs={{0,1},{1,2},{2,3},{3,4},{4,5},{5,6},{6,7},{7,8},{8,9},{9,10},{10,1... | collective-permute-start | bytes 663560
  1399.3 24.8 %collective-permute-start.3 = (f32[36,3456]{1,0:T(8,128)S(1)}, f32[36,3456]{1,0:T(8,128)}, u32[]{:S(2)}, u32[]{:S(2)}) collective-permute-start(f32[36,3456]{1,0:T(8,128)S(1)} %slice.262), channel_id=1, source_target_pairs={{0,4},{1,5},{2,6},{3,7},{4,8},{5,9},{6,10},{7,11},{8,12},{9,13},{1... | collective-permute-start | bytes 1493000
  (120 other events, 856.0 us)
Sparse Core Ops, SparseCore 0:
  10.3 59.8 all-gather.13
  73.0 57.4 all-gather.27
  132.7 58.8 all-gather.17
  194.3 78.7 all-gather.25
  275.8 117.4 all-gather.23
  394.7 129.6 all-gather.15
  526.0 130.9 all-gather.19
  659.2 123.2 reduce-scatter.20
  785.0 123.2 reduce-scatter.18
  916.4 38.0 reduce-scatter.16
  968.7 94.9 reduce-scatter.14
  1067.4 86.9 all-gather.21
  1159.6 160.6 reduce-scatter.24
  1324.9 137.7 reduce-scatter.22
where the time goes:
time: 1480 us; the launch traced here: 1470 us
  matrix products  411 us (28%)
  blocking collectives  368 us (25%)
  waiting for transfers between devices  334 us (23%)
  local copies, waits for them, and re-layouts  160 us (11%)
  other arithmetic  152 us (10%)
  starting transfers between devices  25.5 us (2%)
  between operations  19.7 us (1%)
    unnamed x4, blocking collectives  333 us
    all_gather x1, waiting for transfers between devices, shards(): lax.all_gather(mod_weight, ('row', 'col'), axis=0, tiled=True)  108 us
    unnamed x318, local copies, waits for them, and re-layouts  102 us
    dot_general x4, matrix products, against(): lax.dot_general(left, right, (((1,), (1,)), ((), ())), preferred_element_...  85.6 us
    all_gather x1, waiting for transfers between devices, shards(): lax.all_gather(qkv_weight, ('row', 'col'), axis=0, tiled=True)  73.2 us
    all_gather x1, waiting for transfers between devices, shards(): lax.all_gather(up_weight, 'col', axis=1, tiled=True)  59.5 us
    dot_general x8, matrix products, attend_row_back(): jnp.einsum('qhd,khd->hqk', grad_block, values, preferred_element_type=jnp...  50.4 us
    dot_general x4, matrix products, cross(): lax.dot_general(left, right, (((0,), (0,)), ((), ())), preferred_element_...  49.7 us
  transfers between devices with their start and end apart: 22, of which 9 were waited for; matrix products, arithmetic and copies ran while one was open for 61% of the time, Pallas kernels for 0%

commit v1 on v0

--- a/solution.py
+++ b/solution.py
@@ -1,6 +1,10 @@
+import functools
+
 import jax
 import jax.numpy as jnp
 from jax import lax
+from jax.experimental import pallas as pl
+from jax.experimental.pallas import tpu as pltpu
 from jax.sharding import PartitionSpec as P
 
 H = 16
@@ -167,7 +171,320 @@
     return stacked.reshape(pack, 3 * H * HD).astype(jnp.bfloat16)
 
 
+BOTH = ("row", "col")
+MESH = pl.DeviceIdType.MESH
+BF = jnp.bfloat16
+F32 = jnp.float32
+
+
+def place():
+    col = lax.axis_index("col")
+    return lax.axis_index("row"), col // 4, lax.rem(col // 2, 2), lax.rem(col, 2)
+
+
+def device(y, z, x, c):
+    return (y, z * 4 + x * 2 + c)
+
+
+def peers():
+    y, z, x, c = place()
+    along = [device(y, lax.rem(z + k, 4), x, c) for k in (1, 2, 3)]
+    return along + [device(1 - y, z, x, c), device(y, z, 1 - x, c), device(y, z, x, 1 - c)]
+
+
+def greet():
+    barrier = pltpu.get_barrier_semaphore()
+    for peer in peers():
+        pl.semaphore_signal(barrier, inc=1, device_id=peer, device_id_type=MESH)
+    pl.semaphore_wait(barrier, 6)
+
+
+class Route:
+    def __init__(self, sems, base):
+        self.send, self.recv = sems
+        self.base = base
+        y, z, x, c = place()
+        self.y, self.z, self.x, self.c = y, z, x, c
+        ya, xa = y + c * (1 - 2 * y), x + (1 - c) * (1 - 2 * x)
+        yb, xb = y + (1 - c) * (1 - 2 * y), x + c * (1 - 2 * x)
+        self.lines = [(y, x), (ya, xa), (yb, xb), (1 - y, 1 - x)]
+        self.first = device(ya, z, xa, c)
+        self.second = device(yb, z, xb, c)
+        self.sibling = device(y, z, x, 1 - c)
+
+    def along(self, k):
+        return device(self.y, lax.rem(self.z + k, 4), self.x, self.c)
+
+    def copy(self, i, src, dst, to):
+        return pltpu.make_async_remote_copy(
+            src_ref=src,
+            dst_ref=dst,
+            send_sem=self.send.at[self.base + i],
+            recv_sem=self.recv.at[self.base + i],
+            device_id=to,
+            device_id_type=MESH,
+        )
+
+
+GATHER_SEMS = 11
+
+
+class Gather(Route):
+    def __init__(self, src, dst, sems, base):
+        super().__init__(sems, base)
+        self.src, self.dst = src, dst
+        own = dst(self.y, self.z, self.x, self.c)
+        self.local = pltpu.make_async_copy(src, own, self.send.at[base + 10])
+        self.stage1 = [self.copy(k - 1, src, own, self.along(k)) for k in (1, 2, 3)]
+        line = [dst(yy, slice(None), xx, self.c) for yy, xx in self.lines]
+        self.stage2 = self.copy(3, line[0], line[0], self.first)
+        self.stage3 = [self.copy(4 + w, line[w], line[w], self.second) for w in range(2)]
+        self.stage4 = [self.copy(6 + w, line[w], line[w], self.sibling) for w in range(4)]
+
+    def step(self, s):
+        if s == 0:
+            self.local.start()
+            for copy in self.stage1:
+                copy.start()
+        elif s == 1:
+            self.local.wait()
+            for copy in self.stage1:
+                copy.wait_recv()
+            self.stage2.start()
+            self.stage3[0].start()
+            self.stage4[0].start()
+        elif s == 2:
+            self.stage2.wait_recv()
+            self.stage3[1].start()
+            self.stage4[1].start()
+        elif s == 3:
+            for copy in self.stage3:
+                copy.wait_recv()
+            self.stage4[2].start()
+            self.stage4[3].start()
+        elif s == 4:
+            for copy in self.stage4:
+                copy.wait_recv()
+
+    def finish(self):
+        for copy in self.stage1 + [self.stage2] + self.stage3 + self.stage4:
+            copy.wait_send()
+
+
+def gather_kernel(parts, qkv, out, mlp, all_qkv, all_out, all_mlp, send, recv):
+    chunks = []
+
+    def add(src, dst):
+        chunks.append(Gather(src, dst, (send, recv), GATHER_SEMS * len(chunks)))
+
+    greet()
+    width = out.shape[1]
+    for j in range(3):
+        cut = pl.ds(width * j, width)
+        add(qkv.at[:, cut], lambda a, b, c, d, cut=cut: all_qkv.at[a, b, c, d, :, cut])
+    add(out, lambda a, b, c, d: all_out.at[a, b, c, d])
+    depth = mlp.shape[0] // parts
+    for j in range(parts):
+        cut = pl.ds(depth * j, depth)
+        add(mlp.at[cut], lambda a, b, c, d, cut=cut: all_mlp.at[a, b, c, d, cut])
+    count = len(chunks)
+    chunks[0].step(0)
+    for t in range(count + 4):
+        for s in range(5):
+            if 0 <= t + 1 - s < count and not (t + 1 - s == 0 and s == 0):
+                chunks[t + 1 - s].step(s)
+    for chunk in chunks:
+        chunk.finish()
+
+
+def gather_weights(qkv, out, mlp):
+    parts = 6
+    sems = GATHER_SEMS * (4 + parts)
+    shapes = [jax.ShapeDtypeStruct((2, 4, 2, 2) + a.shape, a.dtype) for a in (qkv, out, mlp)]
+    return pl.pallas_call(
+        functools.partial(gather_kernel, parts),
+        out_shape=shapes,
+        in_specs=[pl.BlockSpec(memory_space=pl.ANY)] * 3,
+        out_specs=[pl.BlockSpec(memory_space=pl.ANY)] * 3,
+        scratch_shapes=[pltpu.SemaphoreType.DMA((sems,)), pltpu.SemaphoreType.DMA((sems,))],
+        compiler_params=pltpu.CompilerParams(collective_id=0, has_side_effects=True),
+    )(qkv, out, mlp)
+
+
 def shards(
+    tokens,
+    lengths,
+    condition,
+    keep_mask,
+    group_mask,
+    qkv_weight,
+    out_weight,
+    mod_weight,
+    out_bias,
+    mod_bias,
+    up_weight,
+    up_bias,
+    down_weight,
+    down_bias,
+    cotangent,
+):
+    rows, pack, width = tokens.shape
+    slots = lengths.shape[1]
+    groups = group_mask.shape[2]
+    count = rows * pack
+    devices = lax.axis_size(BOTH)
+    position = lax.axis_index(BOTH)
+    side = lax.axis_index("row")
+    share = width // devices
+    half = up_weight.shape[0]
+    silu_cond = jax.nn.silu(condition.astype(jnp.float32)).astype(jnp.bfloat16).reshape(rows * slots, width)
+    small = jnp.concatenate([silu_cond.reshape(-1), out_bias, mod_bias, up_bias, down_bias])[None]
+    smalls = lax.all_gather(small, BOTH, axis=0, tiled=True)
+    all_cond = smalls[:, : slots * width].reshape(devices * slots, width)
+    at = slots * width
+    biases = []
+    for part in (out_bias, mod_bias, up_bias, down_bias):
+        biases.append(smalls[:, at : at + part.shape[0]].reshape(-1))
+        at += part.shape[0]
+    out_bias_full, mod_bias_full, up_bias_full, down_bias_full = biases
+    cond_columns = lax.dynamic_slice_in_dim(all_cond, position * share, share, 1)
+    mod_parts = jnp.dot(cond_columns, mod_weight, preferred_element_type=jnp.float32)
+    mods = lax.psum_scatter(mod_parts, BOTH, scatter_dimension=0, tiled=True)
+    up_turned = up_weight.T
+    message = jnp.where(
+        side == 0,
+        jnp.concatenate([up_turned, down_weight], axis=1),
+        jnp.concatenate([down_weight, up_turned], axis=1),
+    )
+    all_qkv, all_out, all_mlp = gather_weights(qkv_weight, out_weight, message)
+    qkv_full = all_qkv.reshape(width, 3 * width)
+    out_full = all_out.reshape(width, width)
+    low, high = all_mlp.reshape(2, -1, width)
+    up_full = jnp.concatenate([low[:, :half], high[:, half:]], axis=1)
+    down_full = jnp.concatenate([low[:, half:], high[:, :half]], axis=1)
+    hidden_units = up_full.shape[0]
+    group_width = hidden_units // groups
+    ends = jnp.cumsum(lengths, axis=1)
+    places = jnp.arange(pack, dtype=jnp.int32)
+    crop = jnp.sum((places[None, :, None] >= ends[:, None, :]).astype(jnp.int32), axis=2)
+    valid = (crop < slots).astype(jnp.float32).reshape(count, 1)
+    keeps = keep_mask.reshape(count, 1).astype(jnp.float32)
+    mods = mods + mod_bias_full.astype(jnp.float32)
+    mods = mods.reshape(rows, slots, 6 * width)
+    per_token = per_crop(mods, crop, slots).reshape(count, 6 * width)
+    shift_one, scale_one, gate_one, shift_two, scale_two, gate_two = jnp.split(per_token, 6, axis=1)
+    channel = per_crop(group_mask.astype(jnp.float32), crop, slots).reshape(count, groups, 1)
+    inputs = tokens.reshape(count, width).astype(jnp.float32)
+    normal_one, inverse_one = normalize(inputs)
+    first_in = (normal_one * (1.0 + scale_one) + shift_one).astype(jnp.bfloat16)
+    projected = jnp.dot(first_in, qkv_full, preferred_element_type=jnp.float32).astype(jnp.bfloat16)
+    packed_rows = projected.reshape(rows, pack, 3 * width)
+    heads_rows, sums_rows = lax.map(lambda item: attend_row(item[0], item[1]), (packed_rows, crop))
+    heads_out = heads_rows.reshape(count, width)
+    attn = jnp.dot(heads_out, out_full, preferred_element_type=jnp.float32) + out_bias_full.astype(
+        jnp.float32
+    )
+    resid = inputs + gate_one * attn
+    normal_two, inverse_two = normalize(resid)
+    second_in = (normal_two * (1.0 + scale_two) + shift_two).astype(jnp.bfloat16)
+    pre = against(second_in, up_full) + up_bias_full.astype(
+        jnp.float32
+    )
+    activated, gelu_pullback = jax.vjp(gelu_tanh, pre)
+    hidden = (
+        (activated.reshape(count, groups, group_width) * channel)
+        .reshape(count, hidden_units)
+        .astype(jnp.bfloat16)
+    )
+    mlp_out = jnp.dot(
+        hidden, down_full, preferred_element_type=jnp.float32
+    ) + down_bias_full.astype(jnp.float32)
+    final = resid + keeps * gate_two * mlp_out
+    block_out = (valid * final).astype(jnp.bfloat16).reshape(rows, pack, width)
+    grad_final = valid * cotangent.reshape(count, width).astype(jnp.float32)
+    grad_mlp = (keeps * gate_two * grad_final).astype(jnp.bfloat16)
+    grad_gate_two = keeps * grad_final * mlp_out
+    grad_down = cross(hidden, grad_mlp)
+    grad_downbias = jnp.sum(grad_mlp.astype(jnp.float32), axis=0)
+    grad_hidden = against(grad_mlp, down_full)
+    grad_masked = (grad_hidden.reshape(count, groups, group_width) * channel).reshape(
+        count, hidden_units
+    )
+    grad_pre = gelu_pullback(grad_masked)[0].astype(jnp.bfloat16)
+    grad_up = cross(grad_pre, second_in)
+    grad_upbias = jnp.sum(grad_pre.astype(jnp.float32), axis=0)
+    grad_second = jnp.dot(grad_pre, up_full, preferred_element_type=jnp.float32)
+    grad_resid = grad_final + norm_back(grad_second * (1.0 + scale_two), normal_two, inverse_two)
+    grad_attn = (gate_one * grad_resid).astype(jnp.bfloat16)
+    grad_gate_one = grad_resid * attn
+    grad_out = cross(heads_out, grad_attn)
+    grad_outbias = jnp.sum(grad_attn.astype(jnp.float32), axis=0)
+    grad_heads = against(grad_attn, out_full).astype(jnp.bfloat16).reshape(rows, pack, width)
+    low = jnp.concatenate([grad_up[:, :half], grad_down[:, :half]], axis=1)
+    high = jnp.concatenate([grad_up[:, half:], grad_down[:, half:]], axis=1)
+    grad_message = jnp.concatenate([low, high], axis=0).astype(jnp.bfloat16)
+    grad_mine = lax.psum_scatter(grad_message, BOTH, scatter_dimension=0, tiled=True).astype(jnp.float32)
+    grad_up_shard = grad_mine[:, :half].T
+    grad_down_shard = grad_mine[:, half:]
+    grad_projected = lax.map(
+        lambda item: attend_row_back(item[0], item[1], item[2], item[3]),
+        (packed_rows, crop, sums_rows, grad_heads),
+    )
+    grad_projected = grad_projected.reshape(count, 3 * width)
+    grad_qkv = cross(first_in, grad_projected)
+    grad_first = against(grad_projected, qkv_full)
+    grad_tokens = grad_resid + norm_back(grad_first * (1.0 + scale_one), normal_one, inverse_one)
+    grad_blocks = [
+        grad_first,
+        grad_first * normal_one,
+        grad_gate_one,
+        grad_second,
+        grad_second * normal_two,
+        grad_gate_two,
+    ]
+    grad_mods = jnp.concatenate(
+        [crop_sums(block.reshape(rows, pack, width), crop, slots) for block in grad_blocks], axis=2
+    )
+    grad_mods = grad_mods.reshape(rows * slots, 6 * width)
+    grad_qkv_shard = lax.psum_scatter(
+        grad_qkv.astype(jnp.bfloat16), BOTH, scatter_dimension=0, tiled=True
+    ).astype(jnp.float32)
+    grad_out_shard = lax.psum_scatter(
+        grad_out.astype(jnp.bfloat16), BOTH, scatter_dimension=0, tiled=True
+    ).astype(jnp.float32)
+    own_bias = jnp.concatenate([grad_outbias, grad_upbias, grad_downbias])[None]
+    last = jnp.concatenate([grad_mods, own_bias], axis=0).astype(jnp.bfloat16)[None]
+    lasts = lax.all_gather(last, BOTH, axis=0, tiled=True)
+    all_grad_mods = lasts[:, :-1].reshape(-1, 6 * width)
+    grad_mod_shard = cross(cond_columns, all_grad_mods)
+    mod_share = 6 * width // devices
+    grad_modbias_shard = jnp.sum(
+        lax.dynamic_slice_in_dim(all_grad_mods, position * mod_share, mod_share, 1).astype(jnp.float32), axis=0
+    )
+    bias_sums = []
+    at = 0
+    for part in (out_bias, up_bias, down_bias):
+        size = part.shape[0]
+        mine = lax.dynamic_slice_in_dim(lasts[:, -1], at + position * size, size, 1)
+        bias_sums.append(jnp.sum(mine.astype(jnp.float32), axis=0))
+        at += size * devices
+    grad_outbias_shard, grad_upbias_shard, grad_downbias_shard = bias_sums
+    return (
+        block_out,
+        grad_tokens.reshape(rows, pack, width),
+        grad_qkv_shard,
+        grad_out_shard,
+        grad_mod_shard,
+        grad_outbias_shard,
+        grad_modbias_shard,
+        grad_up_shard,
+        grad_upbias_shard,
+        grad_down_shard,
+        grad_downbias_shard,
+    )
+
+
+def shards_general(
     tokens,
     lengths,
     condition,
@@ -387,8 +704,9 @@
         P(("row", "col")),
         P(("row", "col"), None, None),
     )
+    fitting = dict(mesh.shape) == {"row": 2, "col": 16}
     return jax.shard_map(
-        shards,
+        shards if fitting else shards_general,
         mesh=mesh,
         in_specs=placed,
         out_specs=(

time: 1480 us -> 1400 us (0.946)
  blocking collectives: 368 us -> 195 us
  Pallas kernels: 0 us -> 154 us
  waiting for transfers between devices: 334 us -> 218 us
  starting transfers between devices: 25.5 us -> 65.5 us
  local copies, waits for them, and re-layouts: 160 us -> 186 us
  matrix products: 411 us -> 387 us
    all_gather x8 -> x1, waiting for transfers between devices: 290 us -> 0.01 us  [shards(): lasts = lax.all_gather(last, BOTH, axis=0, tiled=True)]
    unnamed x24 -> x23, waiting for transfers between devices: 38.4 us -> 218 us
    pallas_call x0 -> x1, Pallas kernels: none -> 154 us  [gather_weights(): pl.pallas_call(functools.partial(gather_kernel, parts), out_shape=shapes,...]
    unnamed x4 -> x1, blocking collectives: 333 us -> 195 us
    unnamed x10 -> x19, starting transfers between devices: 25.1 us -> 65.3 us
    slice x0 -> x6, local copies, waits for them, and re-layouts: none -> 35.9 us  [the longest x2 17.4 us: shards(): low = jnp.concatenate([grad_up[:, :half], grad_down[:, :half]], axis=1)]
    all_gather x1 -> x0, blocking collectives: 35.2 us -> none  [shards(): lax.all_gather(cond_values.astype(jnp.bfloat16), ('row', 'col'), axis=0,...]
    unnamed x318 -> x260, local copies, waits for them, and re-layouts: 102 us -> 73 us
  transfers between devices with their start and end apart: 22 -> 20, of which waited for: 9 -> 3; matrix products, arithmetic and copies ran while one was open for 61% -> 29% of each run, Pallas kernels for 0% -> 11%
where the time goes in v1:
time: 1400 us; the launch traced here: 1380 us
  matrix products  387 us (28%)
  waiting for transfers between devices  218 us (16%)
  blocking collectives  195 us (14%)
  local copies, waits for them, and re-layouts  186 us (13%)
  other arithmetic  164 us (12%)
  Pallas kernels  154 us (11%)
  starting transfers between devices  65.5 us (5%)
  between operations  15.9 us (1%)
    unnamed x23, waiting for transfers between devices  218 us
    unnamed x1, blocking collectives  195 us
    pallas_call x1, Pallas kernels, gather_weights(): pl.pallas_call(functools.partial(gather_kernel, parts), out_shape=shapes,...  154 us
    dot_general x4, matrix products, against(): lax.dot_general(left, right, (((1,), (1,)), ((), ())), preferred_element_...  95.4 us
    unnamed x260, local copies, waits for them, and re-layouts  73 us
    unnamed x19, starting transfers between devices  65.3 us
    dot_general x5, matrix products, cross(): lax.dot_general(left, right, (((0,), (0,)), ((), ())), preferred_element_...  54 us
    dot_general x8, matrix products, attend_row_back(): jnp.einsum('qhd,khd->hqk', grad_block, values, preferred_element_type=jnp...  49.3 us
  transfers between devices with their start and end apart: 20, of which 3 were waited for; matrix products, arithmetic and copies ran while one was open for 29% of the time, Pallas kernels for 11%

profile of v1, /device:TPU:19, one launch (start us, length us, event | category | flops | bytes accessed | tf_op | source)
XLA Modules:
  0.0 1384.9 jit_solution(14467878558774615683)
XLA Ops:
  22.5 153.8 %shard_map.230 = (bf16[2,4,2,2,36,3456]{5,4,3,2,1,0:T(8,128)(2,1)}, bf16[2,4,2,2,36,1152]{5,4,3,2,1,0:T(8,128)(2,1)}, bf16[2,4,2,2,288,1152]{5,4,3,2,1,0:T(8,128)(2,1)}) custom-call(bf16[36,3456]{1,0:T(8,128)(2,1)} %qkv.1, bf16[36,1152]{1,0:T(8,128)(2,1)} %out.1, bf16[288,1152]{1,0:T(8,128)(2,1)} %maximum_select_fusion.mlp), custom_call_target="tpu_custom_call" | custom-call | tf_op jit(solution)/shard_map/pallas_call | solution.py:304
  176.4 11.9 fusion.190
  188.3 15.0 %fusion.193 = (bf16[4608,576]{1,0:T(8,128)(2,1)}, bf16[4608,576]{1,0:T(8,128)(2,1)}, bf16[4608,576]{1,0:T(8,128)(2,1)}, bf16[4608,576]{1,0:T(8,128)(2,1)}) fusion(bf16[4608,1152]{1,0:T(8,128)(2,1)S(1)} %bitcast.377, bf16[4608,1152]{1,0:T(8,128)(2,1)} %bitcast.378), kind=kLoop, calls=%fused_computation.345 | loop fusion | bytes 42467328 | tf_op jit(solution)/shard_map/slice | solution.py:364
  203.4 8.8 mul.448
  212.2 18.7 %copy.65 = f32[1024,4608]{1,0:T(8,128)} copy(f32[1024,4608]{0,1:T(8,128)} %bitcast.330) | data formatting | bytes 37748736 | tf_op jit(solution)/shard_map/mul | solution.py:395
  230.9 12.6 reshape.693
  252.6 136.7 %all-reduce.12.cloned.1.call-done = f32[96,6912]{1,0:T(8,128)} async-done(((f32[96,6912]{1,0:T(8,128)}), f32[96,6912]{1,0:T(8,128)}) %all-reduce.12.cloned.1.call-update) | async-done | bytes 2654224
  390.7 21.2 %select_add_fusion = f32[1024,6912]{1,0:T(8,128)} fusion(f32[6912]{0:T(1024)S(1)} %get-tuple-element.121, f32[6912]{0:T(1024)S(1)} %get-tuple-element.122, f32[6912]{0:T(1024)S(1)} %get-tuple-element.120, pred[1024]{0:T(1024)(128)(4,1)S(1)} %get-tuple-element.157, pred[1024]{0:T(1024)(128)(4,1)S(1)} %get-tuple-element.158, ...), kind=kLoop, calls=%fused_computation | loop fusion | flops 35389440 | bytes 28397568 | tf_op jit(solution)/shard_map/add | solution.py:71
  417.7 14.6 %convolution_convert_fusion.4 = bf16[1024,3456]{1,0:T(8,128)(2,1)} fusion(bf16[1024,1152]{1,0:T(8,128)(2,1)S(1)} %fusion.36, bf16[1152,3456]{1,0:T(8,128)(2,1)} %reshape.693), kind=kOutput, calls=%fused_computation.68 | convolution fusion | flops 8157265920 | bytes 17399808 | tf_op jit(solution)/shard_map/dot_general | solution.py:380
  432.4 10.3 copy.64
  507.6 5.4 fusion.136
  517.0 10.5 fusion.188
  537.8 28.3 %multiply_convert_fusion = (bf16[1024,4608]{1,0:T(8,128)(2,1)}, f32[1024,4608]{1,0:T(8,128)}) fusion(f32[1024,4608]{1,0:T(8,128)} %copy.65, f32[4608]{0:T(1024)S(1)} %copy-done.70, bf16[1024,1152]{1,0:T(8,128)(2,1)} %fusion.43, bf16[4608,576]{1,0:T(8,128)(2,1)} %get-tuple-element.207, bf16[4608,576]{1,0:T(8,128)(2,1)} %get-tuple-element.151), kind=kOutput, calls=%fused_computation.14 | convolution fusion | flops 10944774144 | bytes 60180480 | tf_op jit(solution)/shard_map/dot_general | solution.py:56
  566.1 36.4 %fusion.204 = (bf16[4608]{0:T(1024)(128)(2,1)}, bf16[1024,4608]{1,0:T(8,128)(2,1)}) fusion(f32[1024,4608]{1,0:T(8,128)} %copy.65, bf16[1024,1152]{1,0:T(8,128)(2,1)S(1)} %copy-done.31, bf16[4608,576]{1,0:T(8,128)(2,1)} %get-tuple-element.208, bf16[4608,576]{1,0:T(8,128)(2,1)} %get-tuple-element.150, f32[1024,4608]{1,0:T(8,128)} %get-tuple-element.185, ...), kind=kOutput, calls=%fused_computation.356 | convolution fusion | flops 11020267520 | bytes 60189696 | tf_op jit(solution)/shard_map/dot_general | solution.py:56
  602.5 23.2 %fusion.84 = (f32[1024,1152]{1,0:T(8,128)}, f32[1024,1152]{1,0:T(8,128)}) fusion(f32[1024,1152]{1,0:T(8,128)} %get-tuple-element.142, f32[1024]{0:T(1024)S(1)} %add_rsqrt_fusion, f32[1024]{0:T(1024)S(1)} %broadcast_multiply_fusion.4, bf16[1024,4608]{1,0:T(8,128)(2,1)} %get-tuple-element.206, bf16[4608,576]{1,0:T(8,128)(2,1)} %get-tuple-element.207, ...), kind=kOutput, calls=%fused_computation.172 | convolution fusion | flops 10896408576 | bytes 34217984 | tf_op jit(solution)/shard_map/dot_general | solution.py:416
  625.8 17.3 %convolution_convert_fusion.1 = bf16[4608,1152]{0,1:T(8,128)(2,1)} fusion(bf16[1024,4608]{1,0:T(8,128)(2,1)} %get-tuple-element.206, bf16[1024,1152]{1,0:T(8,128)(2,1)S(1)} %copy-done.26), kind=kOutput, calls=%fused_computation.7 | convolution fusion | flops 10876944384 | bytes 22413312 | tf_op jit(solution)/shard_map/dot_general | solution.py:40
  643.1 17.3 %convolution_convert_fusion = bf16[4608,1152]{0,1:T(8,128)(2,1)} fusion(bf16[1024,4608]{1,0:T(8,128)(2,1)} %get-tuple-element.184, bf16[1024,1152]{1,0:T(8,128)(2,1)S(1)} %copy-done.32), kind=kOutput, calls=%fused_computation.6 | convolution fusion | flops 10876944384 | bytes 22413312 | tf_op jit(solution)/shard_map/dot_general | solution.py:40
  660.5 31.1 %select_reduce_fusion.8 = (bf16[1152]{0:T(1024)(128)(2,1)S(1)}, bf16[1152]{0:T(1024)(128)(2,1)S(1)}, bf16[1152]{0:T(1024)(128)(2,1)S(1)}, f32[1024]{0:T(1024)S(1...) fusion(f32[1024,1152]{1,0:T(8,128)} %get-tuple-element.187, ...), kind=kOutput, calls=%fused_computation.128 | convolution fusion | flops 10934146048 | bytes 48418560 | tf_op jit(solution)/shard_map/dot_general | solution.py:399
  691.6 10.1 fusion.184
  710.9 6.8 fusion.50
  717.7 7.6 multiply_reduce_fusion
  740.6 6.2 multiply_reduce_fusion.2
  746.9 6.2 multiply_reduce_fusion.3
  765.5 6.2 multiply_reduce_fusion.4
  771.7 6.3 multiply_reduce_fusion.5
  790.6 6.3 multiply_reduce_fusion.6
  796.9 6.2 multiply_reduce_fusion.7
  811.7 8.7 fusion.192
  820.6 6.2 fusion.100
  826.8 5.9 fusion.106
  832.7 5.9 fusion.112
  880.5 25.8 %fusion.182 = (f32[1024]{0:T(1024)S(1)}, f32[1024]{0:T(1024)S(1)}, bf16[1152]{0:T(1024)(128)(2,1)S(1)}, bf16[1152]{0:T(1024)(128)(2,1)S(1)}, bf16[1152]{0:T(1024...) fusion(f32[1024,6912]{1,0:T(8,128)} %select_add_fusion, ...), kind=kOutput, calls=%fused_computation.338 | convolution fusion | flops 8186745856 | bytes 36314368 | tf_op jit(solution)/shard_map/dot_general | solution.py:56
  907.4 8.7 fusion.191
  916.0 21.0 %maximum_maximum_fusion = bf16[9216,1152]{0,1:T(8,128)(2,1)} fusion(bf16[4608,576]{0,1:T(8,128)(2,1)} %get-tuple-element.149, bf16[4608,576]{0,1:T(8,128)(2,1)} %get-tuple-element.147, bf16[4608,576]{0,1:T(8,128)(2,1)} %get-tuple-element.148, bf16[4608,576]{0,1:T(8,128)(2,1)} %get-tuple-element.146), kind=kLoop, calls=%fused_computation.5 | loop fusion | flops 84934656 | bytes 42467328 | tf_op jit(solution)/shard_map/concatenate | solution.py:425
  937.0 25.7 %copy.70 = bf16[9216,1152]{1,0:T(8,128)(2,1)} copy(bf16[9216,1152]{0,1:T(8,128)(2,1)} %maximum_maximum_fusion) | data formatting | bytes 42467328
  964.8 6.3 convolution_convert_fusion.3
  971.2 10.9 convolution_convert_fusion.2
  982.1 194.7 %fusion.183 = (bf16[48,3456]{1,0:T(8,128)(2,1)S(1)}, bf16[48,1152]{1,0:T(8,128)(2,1)S(1)}) fusion(bf16[1152,3456]{1,0:T(8,128)(2,1)} %convolution_convert_fusion.2, bf16[1152,1152]{1,0:T(8,128)(2,1)} %convolution_convert_fusion.3), kind=kCustom, calls=%all-reduce-scatter.2 | all-reduce-scatter fusion | flops 7077889 | bytes 11059200
  1176.8 6.5 collective-permute-start.14
  1185.2 6.6 collective-permute-start.12
  1196.1 34.8 %collective-permute-done.15 = bf16[36,1152]{1,0:T(8,128)(2,1)} collective-permute-done((bf16[36,1152]{1,0:T(8,128)(2,1)S(1)}, bf16[36,1152]{1,0:T(8,128)(2,1)}, u32[]{:S(2)}, u32[]{:S(2)}) %collective-permute-start.15) | collective-permute-done | bytes 82976
  1236.7 9.8 collective-permute-start.7
  1252.8 7.5 collective-permute-start.4
  1262.3 46.0 %collective-permute-done.7 = bf16[36,3456]{1,0:T(8,128)(2,1)S(1)} collective-permute-done((bf16[36,3456]{1,0:T(8,128)(2,1)S(1)}, bf16[36,3456]{1,0:T(8,128)(2,1)S(1)}, u32[]{:S(2)}, u32[]{:S(2)}) %collective-permute-start.7) | collective-permute-done | bytes 248864
  1312.2 11.0 collective-permute-start
  1323.2 7.9 fusion.41
  1331.1 6.1 concatenate.129
  1338.6 22.6 %concatenate.128 = bf16[420,3456]{1,0:T(8,128)(2,1)S(1)} concatenate(bf16[36,3456]{1,0:T(8,128)(2,1)} %copy-done.52, bf16[48,3456]{1,0:T(8,128)(2,1)} %copy-done.42, bf16[48,3456]{1,0:T(8,128)(2,1)} %copy-done.43, bf16[48,3456]{1,0:T(8,128)(2,1)} %copy-done.44, bf16[48,3456]{1,0:T(8,128)(2,1)} %collective-permute-done.3, bf16[48,3456]{1,0:T(8,128)(2,1)} %collective-permute-done.2, ...), dimensions={0} | concatenate | bytes 5806080
  (457 shorter events, 255.2 us)
Async XLA Ops:
  7.2 240.0 %copy-start = (bf16[36,6912]{1,0:T(8,128)(2,1)S(1)}, bf16[36,6912]{1,0:T(8,128)(2,1)}, u32[]{:S(2)}) copy-start(bf16[36,6912]{1,0:T(8,128)(2,1)} %param.22) | copy-start | bytes 1492996
  7.2 238.5 %all-reduce.10.cloned.1.call-start = ((), (), s32[]{:S(2)}) async-start(), calls=%async_computation.2 | async-start | bytes 499712
  11.9 377.5 %all-reduce.12.cloned.1.call-start = ((), (), s32[]{:S(2)}) async-start(), calls=%async_computation.4 | async-start | bytes 5308416
  16.9 395.0 %copy-start.64 = (f32[1024]{0:T(1024)}, f32[1024]{0:T(1024)S(1)}, u32[]{:S(2)}) copy-start(f32[1024]{0:T(1024)S(1)} %broadcast_multiply_fusion.5) | copy-start | bytes 12292
  19.9 370.7 %copy-start.75 = (pred[1024]{0:T(1024)(128)(4,1)}, pred[1024]{0:T(1024)(128)(4,1)S(1)}, u32[]{:S(2)}) copy-start(pred[1024]{0:T(1024)(128)(4,1)S(1)} %get-tuple-element.157) | copy-start | bytes 3076
  19.9 370.7 %copy-start.78 = (pred[1024]{0:T(1024)(128)(4,1)}, pred[1024]{0:T(1024)(128)(4,1)S(1)}, u32[]{:S(2)}) copy-start(pred[1024]{0:T(1024)(128)(4,1)S(1)} %get-tuple-element.158) | copy-start | bytes 3076
  19.9 370.7 %copy-start.81 = (pred[1024]{0:T(1024)(128)(4,1)}, pred[1024]{0:T(1024)(128)(4,1)S(1)}, u32[]{:S(2)}) copy-start(pred[1024]{0:T(1024)(128)(4,1)S(1)} %get-tuple-element.159) | copy-start | bytes 3076
  247.2 143.5 %copy-start.45 = (bf16[96,1152]{1,0:T(8,128)(2,1)}, bf16[96,1152]{1,0:T(8,128)(2,1)S(1)}, u32[]{:S(2)}) copy-start(bf16[96,1152]{1,0:T(8,128)(2,1)S(1)} %reshape.691) | copy-start | bytes 663556
  249.3 1112.9 %all-gather.3.cloned.1.call-start = ((), (), s32[]{:S(2)}) async-start(), calls=%async_computation.1 | async-start | bytes 1824768 | tf_op jit(solution)/shard_map/all_gather | solution.py:457
  249.5 162.4 %copy-start.68 = (f32[1024]{0:T(1024)}, f32[1024]{0:T(1024)S(1)}, u32[]{:S(2)}) copy-start(f32[1024]{0:T(1024)S(1)} %add_rsqrt_fusion.1) | copy-start | bytes 12292
  390.7 21.2 %copy-start.11 = (bf16[1,1024,1152]{2,1,0:T(8,128)(2,1)S(1)}, bf16[1,1024,1152]{2,1,0:T(8,128)(2,1)}, u32[]{:S(2)}) copy-start(bf16[1,1024,1152]{2,1,0:T(8,128)(2,1)} %param.15) | copy-start | bytes 7077892
  499.6 14.8 %slice-start = ((s8[28311552]{0:T(1024)(128)(4,1)}), s8[4194304]{0:T(1024)(128)(4,1)S(1)}, s32[]{:S(2)}) async-start(s8[28311552]{0:T(1024)(128)(4,1)} %bitcast.304), calls=%async_computation.5 | async-start | bytes 8388608
  499.6 14.8 %slice-start.1 = ((s8[28311552]{0:T(1024)(128)(4,1)}), s8[4194304]{0:T(1024)(128)(4,1)S(1)}, s32[]{:S(2)}) async-start(s8[28311552]{0:T(1024)(128)(4,1)} %bitcast.304), calls=%async_computation.6 | async-start | bytes 8388608
  537.8 28.3 %copy-start.31 = (bf16[1024,1152]{1,0:T(8,128)(2,1)S(1)}, bf16[1024,1152]{1,0:T(8,128)(2,1)}, u32[]{:S(2)}) copy-start(bf16[1024,1152]{1,0:T(8,128)(2,1)} %get-tuple-element.140) | copy-start | bytes 7077892
  602.5 23.2 %copy-start.26 = (bf16[1024,1152]{1,0:T(8,128)(2,1)S(1)}, bf16[1024,1152]{1,0:T(8,128)(2,1)}, u32[]{:S(2)}) copy-start(bf16[1024,1152]{1,0:T(8,128)(2,1)} %fusion.43) | copy-start | bytes 7077892
  625.8 17.3 %copy-start.32 = (bf16[1024,1152]{1,0:T(8,128)(2,1)S(1)}, bf16[1024,1152]{1,0:T(8,128)(2,1)}, u32[]{:S(2)}) copy-start(bf16[1024,1152]{1,0:T(8,128)(2,1)} %get-tuple-element.140) | copy-start | bytes 7077892
  643.1 17.3 %copy-start.17 = (bf16[1,1024,1152]{2,1,0:T(8,128)(2,1)S(1)}, bf16[1,1024,1152]{2,1,0:T(8,128)(2,1)}, u32[]{:S(2)}) copy-start(bf16[1,1024,1152]{2,1,0:T(8,128)(2,1)} %param.29) | copy-start | bytes 7077892
  643.1 17.3 %copy-start.67 = (f32[1024]{0:T(1024)S(1)}, f32[1024]{0:T(1024)}, u32[]{:S(2)}) copy-start(f32[1024]{0:T(1024)} %get-tuple-element.156) | copy-start | bytes 12292
  643.1 17.3 %copy-start.72 = (f32[1,1024]{1,0:T(1,128)S(1)}, f32[1,1024]{1,0:T(1,128)}, u32[]{:S(2)}) copy-start(f32[1,1024]{1,0:T(1,128)} %convert_element_type.304) | copy-start | bytes 12292
  643.1 17.3 %copy-start.76 = (pred[1024]{0:T(1024)(128)(4,1)S(1)}, pred[1024]{0:T(1024)(128)(4,1)}, u32[]{:S(2)}) copy-start(pred[1024]{0:T(1024)(128)(4,1)} %copy-done.75) | copy-start | bytes 3076
  643.1 17.3 %copy-start.79 = (pred[1024]{0:T(1024)(128)(4,1)S(1)}, pred[1024]{0:T(1024)(128)(4,1)}, u32[]{:S(2)}) copy-start(pred[1024]{0:T(1024)(128)(4,1)} %copy-done.78) | copy-start | bytes 3076
  643.1 17.3 %copy-start.82 = (pred[1024]{0:T(1024)(128)(4,1)S(1)}, pred[1024]{0:T(1024)(128)(4,1)}, u32[]{:S(2)}) copy-start(pred[1024]{0:T(1024)(128)(4,1)} %copy-done.81) | copy-start | bytes 3076
  643.1 17.3 %copy-start.84 = (f32[1152]{0:T(1024)S(1)}, f32[1152]{0:T(1024)}, u32[]{:S(2)}) copy-start(f32[1152]{0:T(1024)} %reshape.703) | copy-start | bytes 13828
  710.9 14.4 %copy-start.13 = (bf16[1024,1152]{0,1:T(8,128)(2,1)}, bf16[1024,1152]{0,1:T(8,128)(2,1)S(1)}, u32[]{:S(2)}) copy-start(bf16[1024,1152]{0,1:T(8,128)(2,1)S(1)} %copy.67) | copy-start | bytes 7077892
  710.9 14.4 %slice-start.21 = ((s8[8388608]{0:T(1024)(128)(4,1)}), s8[4194304]{0:T(1024)(128)(4,1)S(1)}, s32[]{:S(2)}) async-start(s8[8388608]{0:T(1024)(128)(4,1)} %bitcast.320), calls=%async_computation.26 | async-start | bytes 8388608
  746.9 15.0 %slice-start.11 = ((s8[8388608]{0:T(1024)(128)(4,1)}), s8[4194304]{0:T(1024)(128)(4,1)S(1)}, s32[]{:S(2)}) async-start(s8[8388608]{0:T(1024)(128)(4,1)} %bitcast.310), calls=%async_computation.16 | async-start | bytes 8388608
  771.7 15.3 %slice-start.7 = ((s8[8388608]{0:T(1024)(128)(4,1)}), s8[4194304]{0:T(1024)(128)(4,1)S(1)}, s32[]{:S(2)}) async-start(s8[8388608]{0:T(1024)(128)(4,1)} %bitcast.306), calls=%async_computation.12 | async-start | bytes 8388608
  820.6 18.1 %slice-start.23 = ((s8[8388608]{0:T(1024)(128)(4,1)}), s8[4194304]{0:T(1024)(128)(4,1)S(1)}, s32[]{:S(2)}) async-start(s8[8388608]{0:T(1024)(128)(4,1)} %bitcast.322), calls=%async_computation.28 | async-start | bytes 8388608
  826.8 15.3 %slice-start.19 = ((s8[8388608]{0:T(1024)(128)(4,1)}), s8[4194304]{0:T(1024)(128)(4,1)S(1)}, s32[]{:S(2)}) async-start(s8[8388608]{0:T(1024)(128)(4,1)} %bitcast.318), calls=%async_computation.24 | async-start | bytes 8388608
  907.3 464.6 %reduce-scatter.8.cloned.1.call-start = ((), (), s32[]{:S(2)}) async-start(), calls=%async_computation.3 | async-start | bytes 21897216
  1176.8 56.0 %collective-permute-start.14 = (bf16[48,1152]{1,0:T(8,128)(2,1)S(1)}, bf16[48,1152]{1,0:T(8,128)(2,1)S(1)}, u32[]{:S(2)}, u32[]{:S(2)}) collective-permute-start(bf16[48,1152]{1,0:T(8,128)(2,1)S(1)} %get-tuple-element.135), channel_id=1, source_target_pairs={{0,7},{1,8},{2,9},{3,10},{4,11},{5,12},{6,13},{7,14},{8,15},{9,16}... | collective-permute-start | bytes 331784
  1183.2 51.5 %collective-permute-start.13 = (bf16[48,1152]{1,0:T(8,128)(2,1)S(1)}, bf16[48,1152]{1,0:T(8,128)(2,1)S(1)}, u32[]{:S(2)}, u32[]{:S(2)}) collective-permute-start(bf16[48,1152]{1,0:T(8,128)(2,1)S(1)} %get-tuple-element.135), channel_id=1, source_target_pairs={{0,6},{1,7},{2,8},{3,9},{4,10},{5,11},{6,12},{7,13},{8,14},{9,15},... | collective-permute-start | bytes 331784
  1185.2 51.5 %collective-permute-start.12 = (bf16[48,1152]{1,0:T(8,128)(2,1)S(1)}, bf16[48,1152]{1,0:T(8,128)(2,1)S(1)}, u32[]{:S(2)}, u32[]{:S(2)}) collective-permute-start(bf16[48,1152]{1,0:T(8,128)(2,1)S(1)} %get-tuple-element.135), channel_id=1, source_target_pairs={{0,5},{1,6},{2,7},{3,8},{4,9},{5,10},{6,11},{7,12},{8,13},{9,14},{... | collective-permute-start | bytes 331784
  1191.8 39.1 %collective-permute-start.15 = (bf16[36,1152]{1,0:T(8,128)(2,1)S(1)}, bf16[36,1152]{1,0:T(8,128)(2,1)}, u32[]{:S(2)}, u32[]{:S(2)}) collective-permute-start(bf16[36,1152]{1,0:T(8,128)(2,1)S(1)} %slice.356), channel_id=1, source_target_pairs={{0,8},{1,9},{2,10},{3,11},{4,12},{5,13},{6,14},{7,15},{8,16},{9,17... | collective-permute-start | bytes 248840
  1194.1 52.4 %collective-permute-start.11 = (bf16[48,1152]{1,0:T(8,128)(2,1)S(1)}, bf16[48,1152]{1,0:T(8,128)(2,1)S(1)}, u32[]{:S(2)}, u32[]{:S(2)}) collective-permute-start(bf16[48,1152]{1,0:T(8,128)(2,1)S(1)} %get-tuple-element.135), channel_id=1, source_target_pairs={{0,4},{1,5},{2,6},{3,7},{4,8},{5,9},{6,10},{7,11},{8,12},{9,13},{1... | collective-permute-start | bytes 331784
  1230.9 19.6 %collective-permute-start.10 = (bf16[48,1152]{1,0:T(8,128)(2,1)S(1)}, bf16[48,1152]{1,0:T(8,128)(2,1)S(1)}, u32[]{:S(2)}, u32[]{:S(2)}) collective-permute-start(bf16[48,1152]{1,0:T(8,128)(2,1)S(1)} %get-tuple-element.135), channel_id=1, source_target_pairs={{0,3},{1,4},{2,5},{3,6},{4,7},{5,8},{6,9},{7,10},{8,11},{9,12},{10... | collective-permute-start | bytes 331784
  1232.8 77.4 %collective-permute-start.6 = (bf16[48,3456]{1,0:T(8,128)(2,1)S(1)}, bf16[48,3456]{1,0:T(8,128)(2,1)S(1)}, u32[]{:S(2)}, u32[]{:S(2)}) collective-permute-start(bf16[48,3456]{1,0:T(8,128)(2,1)S(1)} %get-tuple-element.134), channel_id=1, source_target_pairs={{0,7},{1,8},{2,9},{3,10},{4,11},{5,12},{6,13},{7,14},{8,15},{9,16}... | collective-permute-start | bytes 995336
  1234.8 77.4 %collective-permute-start.5 = (bf16[48,3456]{1,0:T(8,128)(2,1)S(1)}, bf16[48,3456]{1,0:T(8,128)(2,1)S(1)}, u32[]{:S(2)}, u32[]{:S(2)}) collective-permute-start(bf16[48,3456]{1,0:T(8,128)(2,1)S(1)} %get-tuple-element.134), channel_id=1, source_target_pairs={{0,6},{1,7},{2,8},{3,9},{4,10},{5,11},{6,12},{7,13},{8,14},{9,15},... | collective-permute-start | bytes 995336
  1236.7 71.6 %collective-permute-start.7 = (bf16[36,3456]{1,0:T(8,128)(2,1)S(1)}, bf16[36,3456]{1,0:T(8,128)(2,1)S(1)}, u32[]{:S(2)}, u32[]{:S(2)}) collective-permute-start(bf16[36,3456]{1,0:T(8,128)(2,1)S(1)} %slice.355), channel_id=1, source_target_pairs={{0,8},{1,9},{2,10},{3,11},{4,12},{5,13},{6,14},{7,15},{8,16},{9,17... | collective-permute-start | bytes 746504
  1246.5 6.3 collective-permute-start.9
  1250.5 9.8 collective-permute-start.8
  1252.8 85.1 %collective-permute-start.4 = (bf16[48,3456]{1,0:T(8,128)(2,1)S(1)}, bf16[48,3456]{1,0:T(8,128)(2,1)S(1)}, u32[]{:S(2)}, u32[]{:S(2)}) collective-permute-start(bf16[48,3456]{1,0:T(8,128)(2,1)S(1)} %get-tuple-element.134), channel_id=1, source_target_pairs={{0,5},{1,6},{2,7},{3,8},{4,9},{5,10},{6,11},{7,12},{8,13},{9,14},{... | collective-permute-start | bytes 995336
  1260.3 62.9 %copy-start.63 = (bf16[48,1152]{1,0:T(8,128)(2,1)}, bf16[48,1152]{1,0:T(8,128)(2,1)S(1)}, u32[]{:S(2)}) copy-start(bf16[48,1152]{1,0:T(8,128)(2,1)S(1)} %collective-permute-done.8) | copy-start | bytes 331780
  1260.3 77.6 %collective-permute-start.3 = (bf16[48,3456]{1,0:T(8,128)(2,1)S(1)}, bf16[48,3456]{1,0:T(8,128)(2,1)}, u32[]{:S(2)}, u32[]{:S(2)}) collective-permute-start(bf16[48,3456]{1,0:T(8,128)(2,1)S(1)} %get-tuple-element.134), channel_id=1, source_target_pairs={{0,4},{1,5},{2,6},{3,7},{4,8},{5,9},{6,10},{7,11},{8,12},{9,13},{1... | collective-permute-start | bytes 995336
  1308.3 14.9 %copy-start.52 = (bf16[36,3456]{1,0:T(8,128)(2,1)}, bf16[36,3456]{1,0:T(8,128)(2,1)S(1)}, u32[]{:S(2)}) copy-start(bf16[36,3456]{1,0:T(8,128)(2,1)S(1)} %collective-permute-done.7) | copy-start | bytes 746500
  1308.3 29.6 %collective-permute-start.2 = (bf16[48,3456]{1,0:T(8,128)(2,1)S(1)}, bf16[48,3456]{1,0:T(8,128)(2,1)}, u32[]{:S(2)}, u32[]{:S(2)}) collective-permute-start(bf16[48,3456]{1,0:T(8,128)(2,1)S(1)} %get-tuple-element.134), channel_id=1, source_target_pairs={{0,3},{1,4},{2,5},{3,6},{4,7},{5,8},{6,9},{7,10},{8,11},{9,12},{10... | collective-permute-start | bytes 995336
  1310.2 27.7 %collective-permute-start.1 = (bf16[48,3456]{1,0:T(8,128)(2,1)S(1)}, bf16[48,3456]{1,0:T(8,128)(2,1)}, u32[]{:S(2)}, u32[]{:S(2)}) collective-permute-start(bf16[48,3456]{1,0:T(8,128)(2,1)S(1)} %get-tuple-element.134), channel_id=1, source_target_pairs={{0,2},{1,3},{2,4},{3,5},{4,6},{5,7},{6,8},{7,9},{8,10},{9,11},{10,... | collective-permute-start | bytes 995336
  1312.2 26.4 %collective-permute-start = (bf16[48,3456]{1,0:T(8,128)(2,1)S(1)}, bf16[48,3456]{1,0:T(8,128)(2,1)}, u32[]{:S(2)}, u32[]{:S(2)}) collective-permute-start(bf16[48,3456]{1,0:T(8,128)(2,1)S(1)} %get-tuple-element.134), channel_id=1, source_target_pairs={{0,1},{1,2},{2,3},{3,4},{4,5},{5,6},{6,7},{7,8},{8,9},{9,10},{10,1... | collective-permute-start | bytes 995336
  (97 other events, 585.9 us)
Sparse Core Ops, SparseCore 0:
  14.1 138.1 all-reduce.9
  249.4 139.8 all-reduce.11
  907.4 55.2 all-gather.2
  970.1 346.4 reduce-scatter.7
